TPU v7x, 256 devices: a whole 4x4x8 slice. The times are simulated.
256 devices in a mesh: seq: 32 (over z_hi, x, y), ch: 8 (over z_lo, core).
Axes of the slice: x: 4, y: 4, z: 8 (z_hi: 2, z_lo: 4; z = z_hi * 4 + z_lo), core: 2. Of those that a mesh axis runs over, the one named last changes fastest.
Arguments:
- seq_values: bfloat16 [1024, 512, 512], P('ch', 'seq'), may hold values from -6 to 6
- gate_values: bfloat16 [1024, 512, 512], P('ch', 'seq'), may hold values from -6 to 6
- out_grad: bfloat16 [1024, 512, 512], P('ch', 'seq'), may hold values from -6 to 6
- factor_one: bfloat16 [512, 512], replicated, may hold values from -0.25 to 0.25
- factor_two: bfloat16 [512, 512], replicated, may hold values from -0.25 to 0.25
- twiddle: bfloat16 [512, 512], P('seq'), may hold values from 0.3984375 to 1.59375
Outputs:
- values_grad: bfloat16 [1024, 512, 512], P('ch', 'seq')
- gate_grad: bfloat16 [1024, 512, 512], P('ch', 'seq')
- factor_one_grad: float32 [512, 512], P('seq')
- factor_two_grad: float32 [512, 512], P('seq')
- twiddle_grad: float32 [512, 512], P('seq')
All inputs are finite; a program needn't handle non-finite values.
Results may differ from a plain program's by a relative error of at most 0.0064.
Values may be sent and summed in bfloat16 or wider, within the bound.
A program may use at most 64 MiB of HBM per device.

v0:
```python
import jax
import jax.numpy as jnp
from jax import lax
from jax.sharding import PartitionSpec as P


def second_backward(grad_across, gathered, factor_two):
    block_grad = jnp.einsum(
        "cjr,jb->cbr", grad_across, factor_two, preferred_element_type=jnp.float32
    ).astype(jnp.bfloat16)
    second_part = jnp.einsum(
        "cjr,cbr->jb", grad_across, gathered, preferred_element_type=jnp.float32
    )
    return (block_grad, second_part)


def body(seq_values, gate_values, out_grad, factor_one, factor_two, twiddle):
    f32 = jnp.float32
    width = seq_values.shape[0] * lax.axis_size("ch")
    blocks = factor_two.shape[0]
    block_len = factor_one.shape[0]
    twiddle_f = twiddle.astype(f32)
    pre_twiddle = jnp.einsum("cbs,rs->cbr", seq_values, factor_one, preferred_element_type=f32)
    mixed_first = (pre_twiddle * twiddle_f[None]).astype(jnp.bfloat16)
    pieces = lax.all_to_all(mixed_first, "seq", split_axis=2, concat_axis=1, tiled=True)
    product = jnp.einsum("cbr,jb->cjr", pieces, factor_two, preferred_element_type=f32)
    mixed_across = product.astype(jnp.bfloat16)
    mixed = lax.all_to_all(mixed_across, "seq", split_axis=1, concat_axis=2, tiled=True)
    gate_grad = (out_grad.astype(f32) * mixed.astype(f32)).astype(jnp.bfloat16)
    mixed_grad = (gate_values.astype(f32) * out_grad.astype(f32)).astype(jnp.bfloat16)
    grad_across = lax.all_to_all(mixed_grad, "seq", split_axis=2, concat_axis=1, tiled=True)
    block_grad, second_part = second_backward(grad_across, pieces, factor_two)
    first_grad = lax.all_to_all(block_grad, "seq", split_axis=1, concat_axis=2, tiled=True)
    first_grad_f = first_grad.astype(f32)
    scaled_grad = (first_grad_f * twiddle_f[None]).astype(jnp.bfloat16)
    twiddle_part = jnp.sum(first_grad_f * pre_twiddle, axis=0)
    values_grad = jnp.einsum(
        "cbr,rs->cbs", scaled_grad, factor_one, preferred_element_type=f32
    ).astype(jnp.bfloat16)
    first_part = jnp.einsum("cbr,cbs->rs", scaled_grad, seq_values, preferred_element_type=f32)
    one_total, two_total, twiddle_total = lax.psum((first_part, second_part, twiddle_part), "ch")
    one_rows, two_rows = (
        lax.psum_scatter(one_total, "seq", scatter_dimension=0, tiled=True),
        lax.psum_scatter(two_total, "seq", scatter_dimension=0, tiled=True),
    )
    factor_one_grad = one_rows * (1.0 / (width * blocks) ** 0.5)
    factor_two_grad = two_rows * (1.0 / (width * block_len) ** 0.5)
    twiddle_grad = twiddle_total * (1.0 / width**0.5)
    return (values_grad, gate_grad, factor_one_grad, factor_two_grad, twiddle_grad)


def solution(mesh):
    return jax.shard_map(
        body,
        mesh=mesh,
        in_specs=(
            P("ch", "seq", None),
            P("ch", "seq", None),
            P("ch", "seq", None),
            P(),
            P(),
            P("seq", None),
        ),
        out_specs=(
            P("ch", "seq", None),
            P("ch", "seq", None),
            P("seq", None),
            P("seq", None),
            P("seq", None),
        ),
        check_vma=False,
    )
```

profile of v0, /device:TPU:1, one launch (start us, length us, event | category | flops | bytes accessed | tf_op | source)
XLA Modules:
  0.0 726.8 jit_solution(346508620219101652)
XLA Ops:
  7.2 3.5 copy.41
  10.7 4.5 copy.40
  18.7 50.6 %all_to_all.54 = bf16[128,16,512]{0,1,2:T(8,128)(2,1)S(1)} all-to-all(bf16[128,16,512]{0,1,2:T(8,128)(2,1)S(1)} %copy.42), channel_id=1, replica_groups=mesh['seq'=32,'ch'=8] {'seq'}, dimensions={2} | all-to-all | bytes 4194304 | tf_op jit(solution)/shard_map/all_to_all | solution.py:31
  71.3 2.7 convert_bitcast_fusion.3
  73.9 4.5 copy.46
  78.4 4.9 all-to-all-start.1
  83.4 20.0 %all-to-all-done.1 = bf16[128,512,16]{0,2,1:T(8,128)(2,1)} async-done(((bf16[128,512,16]{0,2,1:T(8,128)(2,1)}), bf16[128,512,16]{0,2,1:T(8,128)(2,1)}, u32[]{:S(2)}, u32[]{:S(2)}) %all-to-all-start.1) | async-done | bytes 2097184 | tf_op jit(solution)/shard_map/all_to_all | solution.py:33
  107.9 5.4 copy.48
  113.3 7.5 %multiply_reduce_fusion = (f32[16,512]{1,0:T(8,128)}, bf16[128,16,512]{2,0,1:T(8,128)(2,1)}) fusion(f32[128,16,512]{2,0,1:T(8,128)} %copy.48, f32[16,512]{1,0:T(8,128)S(1)} %convert_element_type.70, bf16[512,512]{1,0:T(8,128)(2,1)S(1)} %copy-done, bf16[128,16,512]{2,1,0:T(8,128)(2,1)} %param.6), kind=kOutput, calls=%fused_computation.6 | convolution fusion | flops 1077927936 | bytes 8978432 | tf_op jit(solution)/shard_map/cbs,rs->cbr/dot_general | solution.py:23
  120.8 4.5 copy.50
  125.3 5.7 all-to-all-start.2
  131.2 7.0 fusion.9
  138.2 14.5 %all-to-all-done.2 = bf16[128,16,512]{0,1,2:T(8,128)(2,1)} async-done(((bf16[128,16,512]{0,1,2:T(8,128)(2,1)}), bf16[128,16,512]{0,1,2:T(8,128)(2,1)}, u32[]{:S(2)}, u32[]{:S(2)}) %all-to-all-start.2) | async-done | bytes 2097184 | tf_op jit(solution)/shard_map/all_to_all | solution.py:25
  152.7 3.5 copy.52
  156.1 4.3 copy.53
  160.4 4.2 convert_bitcast_fusion.2
  164.6 4.6 copy.54
  169.2 9.0 %all-to-all-start.3 = ((bf16[128,512,16]{0,2,1:T(8,128)(2,1)}), bf16[128,512,16]{0,2,1:T(8,128)(2,1)}, u32[]{:S(2)}, u32[]{:S(2)}) async-start(bf16[128,512,16]{0,2,1:T(8,128)(2,1)} %copy.54), calls=%async_computation.3 | async-start | bytes 4194304 | tf_op jit(solution)/shard_map/all_to_all | solution.py:28
  178.3 4.4 fusion.12
  182.8 212.4 %reduce-scatter.3.cloned.1.call-done = f32[16,512]{1,0:T(8,128)} async-done(((f32[512,512]{1,0:T(8,128)}), f32[16,512]{1,0:T(8,128)}) %reduce-scatter.3.cloned.1.call-update) | async-done | bytes 32784 | tf_op jit(solution)/shard_map/reduce_scatter | solution.py:43
  395.2 227.6 %reduce-scatter.5.cloned.1.call-done = f32[16,512]{1,0:T(8,128)} async-done(((f32[512,512]{1,0:T(8,128)}), f32[16,512]{1,0:T(8,128)}) %reduce-scatter.5.cloned.1.call-update) | async-done | bytes 32784 | tf_op jit(solution)/shard_map/reduce_scatter | solution.py:44
  622.8 3.4 convolution_convert_fusion
  628.7 79.8 %all-reduce.3.cloned.1.call-done = (f32[16,512]{1,0:T(8,128)}, f32[16,512]{1,0:T(8,128)}, f32[16,512]{1,0:T(8,128)}) async-done(((f32[16,512]{1,0:T(8,128)}, f32[16,512]{1,0:T(8,128)}, f32[16,512]{1,0:T(8,128)}), (f32[16,512]{1,0:T(8,128)}, f32[16,512]{1,0:T(8,128)}, f32[16,512]{1,0:T(8,128)})) %all-reduce.3.cloned.1.call-update) | async-done | bytes 98320 | tf_op jit(solution)/shard_map/psum | solution.py:41
  715.7 4.5 copy.62
  (27 shorter events, 20.0 us)
Async XLA Ops:
  7.2 106.1 %copy-start = (bf16[512,512]{1,0:T(8,128)(2,1)S(1)}, bf16[512,512]{1,0:T(8,128)(2,1)}, u32[]{:S(2)}) copy-start(bf16[512,512]{1,0:T(8,128)(2,1)} %param.9) | copy-start | bytes 1572868
  69.4 1.9 copy-start.2
  69.9 1.4 copy-start.1
  78.4 4.9 copy-start.3
  78.4 24.9 %all-to-all-start.1 = ((bf16[128,512,16]{0,2,1:T(8,128)(2,1)}), bf16[128,512,16]{0,2,1:T(8,128)(2,1)}, u32[]{:S(2)}, u32[]{:S(2)}) async-start(bf16[128,512,16]{0,2,1:T(8,128)(2,1)} %copy.46), calls=%async_computation.1 | async-start | bytes 4194304 | tf_op jit(solution)/shard_map/all_to_all | solution.py:33
  125.3 27.4 %all-to-all-start.2 = ((bf16[128,16,512]{0,1,2:T(8,128)(2,1)}), bf16[128,16,512]{0,1,2:T(8,128)(2,1)}, u32[]{:S(2)}, u32[]{:S(2)}) async-start(bf16[128,16,512]{0,1,2:T(8,128)(2,1)} %copy.50), calls=%async_computation.2 | async-start | bytes 4194304 | tf_op jit(solution)/shard_map/all_to_all | solution.py:25
  131.0 264.3 %reduce-scatter.3.cloned.1.call-start = ((), (), s32[]{:S(2)}) async-start(), calls=%async_computation.6 | async-start | bytes 1081344 | tf_op jit(solution)/shard_map/reduce_scatter | solution.py:43
  169.2 542.1 %all-to-all-start.3 = ((bf16[128,512,16]{0,2,1:T(8,128)(2,1)}), bf16[128,512,16]{0,2,1:T(8,128)(2,1)}, u32[]{:S(2)}, u32[]{:S(2)}) async-start(bf16[128,512,16]{0,2,1:T(8,128)(2,1)} %copy.54), calls=%async_computation.3 | async-start | bytes 4194304 | tf_op jit(solution)/shard_map/all_to_all | solution.py:28
  178.2 444.6 %reduce-scatter.5.cloned.1.call-start = ((), (), s32[]{:S(2)}) async-start(), calls=%async_computation.7 | async-start | bytes 1081344 | tf_op jit(solution)/shard_map/reduce_scatter | solution.py:44
  182.7 525.8 %all-reduce.3.cloned.1.call-start = ((), (), s32[]{:S(2)}) async-start(), calls=%async_computation.8 | async-start | bytes 196608 | tf_op jit(solution)/shard_map/psum | solution.py:41
Sparse Core Ops, SparseCore 0:
  138.3 256.8 reduce-scatter.2
  398.4 224.2 reduce-scatter.4
  626.2 82.2 all-reduce.2
where the time goes:
time: 729 us; the launch traced here: 727 us
  waiting for transfers between devices  554 us (76%)
  blocking collectives  50.6 us (7%)
  local copies, waits for them, and re-layouts  47.8 us (7%)
  matrix products  29.3 us (4%)
  starting transfers between devices  19.9 us (3%)
  between operations  13.9 us (2%)
  other arithmetic  11 us (2%)
    reduce_scatter x1, waiting for transfers between devices, body(): lax.psum_scatter(two_total, 'seq', scatter_dimension=0, tiled=True)  228 us
    reduce_scatter x1, waiting for transfers between devices, body(): lax.psum_scatter(one_total, 'seq', scatter_dimension=0, tiled=True)  212 us
    psum x1, waiting for transfers between devices, body(): lax.psum((first_part, second_part, twiddle_part), 'ch')  79.8 us
    all_to_all x1, blocking collectives, body(): lax.all_to_all(mixed_grad, 'seq', split_axis=2, concat_axis=1, tiled=True)  50.6 us
    all_to_all x1, waiting for transfers between devices, body(): lax.all_to_all(block_grad, 'seq', split_axis=1, concat_axis=2, tiled=True)  20 us
    unnamed x12, local copies, waits for them, and re-layouts  16.4 us
  transfers between devices with their start and end apart: 6, of which 5 were waited for; matrix products, arithmetic and copies ran while one was open for 5% of the time, Pallas kernels for 0%

commit v1 on v0

v1 whole, which is shorter than its diff:
```python
import functools

import jax
import jax.numpy as jnp
from jax import lax
from jax.experimental import pallas as pl
from jax.experimental.pallas import tpu as pltpu
from jax.sharding import PartitionSpec as P

MESH = pl.DeviceIdType.MESH
NX, NY, ZH, ZL, NC = 4, 4, 2, 4, 2
PLANE = NX * NY
NZ = ZH * ZL
SEQ = ZH * PLANE
STEPS = 4
MG, MF, FG, MX = 0, STEPS, 2 * STEPS, 3 * STEPS
F32 = jnp.float32
BF16 = jnp.bfloat16


def dot(a, b, ca, cb):
    return lax.dot_general(a, b, (((ca,), (cb,)), ((), ())), preferred_element_type=F32)


def kernel(
    scales,
    x_hbm, gate_hbm, og_hbm, one_hbm, two_hbm, tw_hbm,
    vg_hbm, gg_hbm, one_out, two_out, tw_out,
    x_v, gate_v, og_v, one_v, two_v, two_t, tw_v, pre_v,
    out_buf, relay_buf, in_buf, vg_v, gg_v,
    grad_v, sib_v, sum_v, plane_v, zsend_v, zrecv_v,
    tw_part, tw_sib, tw_sum, tw_recv, fin_v,
    load_sem, mat_sem, store_sem,
    z_send, z_recv, own_send, fwd_send, in_recv,
    sib_send, sib_recv, pl_send, pl_recv, zz_send, zz_recv,
    tws_send, tws_recv, twz_send, twz_recv, fin_send, fin_recv,
):
    seq = lax.axis_index("seq")
    ch = lax.axis_index("ch")
    hi, at = seq // PLANE, seq % PLANE
    px, py = at // NY, at % NY
    lo, core = ch // NC, ch % NC
    z = hi * ZL + lo
    other_hi = 1 - hi

    def plane_at(d):
        return ((px + d // NY) % NX) * NY + (py + d % NY) % NY

    def plane_dev(to):
        return (hi * PLANE + to, ch)

    across = (other_hi * PLANE + at, ch)
    sibling = (seq, lo * NC + 1 - core)

    def z_dev(to):
        return ((to // ZL) * PLANE + at, (to % ZL) * NC + core)

    def remote(src, dst, ssem, rsem, dev):
        return pltpu.make_async_remote_copy(
            src_ref=src, dst_ref=dst, send_sem=ssem, recv_sem=rsem,
            device_id=dev, device_id_type=MESH,
        )

    def drain(ref, sem):
        pltpu.make_async_copy(ref, ref, sem).wait()

    def load(n, src, dst, k):
        return pltpu.make_async_copy(src.at[:, k], dst.at[k], load_sem.at[n, k])

    mats = (
        pltpu.make_async_copy(one_hbm, one_v, mat_sem.at[0]),
        pltpu.make_async_copy(tw_hbm, tw_v, mat_sem.at[1]),
        pltpu.make_async_copy(two_hbm, two_v, mat_sem.at[2]),
    )

    for k in range(STEPS):
        load(0, gate_hbm, gate_v, k).start()
        load(1, og_hbm, og_v, k).start()
    mats[0].start()
    mats[1].start()
    for k in range(STEPS):
        load(2, x_hbm, x_v, k).start()
    mats[2].start()

    barrier = pltpu.get_barrier_semaphore()

    @pl.loop(1, PLANE)
    def _(d):
        pl.semaphore_signal(barrier, inc=1, device_id=plane_dev(plane_at(d)), device_id_type=MESH)

    @pl.loop(1, NZ)
    def _(d):
        pl.semaphore_signal(barrier, inc=1, device_id=z_dev((z + d) % NZ), device_id_type=MESH)

    pl.semaphore_signal(barrier, inc=1, device_id=sibling, device_id_type=MESH)
    pl.semaphore_wait(barrier, PLANE - 1 + NZ - 1 + 1)

    def across_copy(i):
        return remote(
            out_buf.at[i, pl.ds(other_hi * PLANE, PLANE)], relay_buf.at[i],
            z_send.at[i], z_recv.at[i], across,
        )

    def send(i):
        across_copy(i).start()

        @pl.loop(1, PLANE)
        def _(d):
            to = plane_at(d)
            remote(
                out_buf.at[i, hi * PLANE + to], in_buf.at[i, seq],
                own_send.at[i], in_recv.at[i], plane_dev(to),
            ).start()

        pltpu.make_async_copy(out_buf.at[i, seq], in_buf.at[i, seq], in_recv.at[i]).start()

    def forward(i):
        across_copy(i).wait_recv()
        origin = other_hi * PLANE + at

        @pl.loop(1, PLANE)
        def _(d):
            to = plane_at(d)
            remote(
                relay_buf.at[i, to], in_buf.at[i, origin],
                fwd_send.at[i], in_recv.at[i], plane_dev(to),
            ).start()

        pltpu.make_async_copy(relay_buf.at[i, at], in_buf.at[i, origin], in_recv.at[i]).start()

    def arrived(i):
        drain(in_buf.at[i], in_recv.at[i])

    def flat(ref):
        return ref.reshape(SEQ * 16, 512)

    def blocks(value):
        return value.reshape(SEQ, 16, 512)

    @pl.loop(0, STEPS)
    def _(k):
        load(0, gate_hbm, gate_v, k).wait()
        load(1, og_hbm, og_v, k).wait()
        out_buf[MG + k] = (gate_v[k].astype(F32) * og_v[k].astype(F32)).astype(BF16)
        send(MG + k)

    mats[0].wait()
    mats[1].wait()

    @pl.loop(0, STEPS)
    def _(k):
        load(2, x_hbm, x_v, k).wait()
        pre = dot(x_v[k].reshape(SEQ * 16, 512), one_v[...], 1, 1)
        pre_v[k] = blocks(pre)
        out_buf[MF + k] = (blocks(pre) * tw_v[...].astype(F32)[None]).astype(BF16)
        send(MF + k)

    mats[2].wait()
    two_t[...] = two_v[...].T
    grad_v[...] = jnp.zeros_like(grad_v)
    tw_part[...] = jnp.zeros_like(tw_part)
    forward(MG)

    @pl.loop(0, STEPS)
    def _(k):
        forward(MG + k + 1)
        arrived(MG + k)
        grad = in_buf[MG + k].reshape(SEQ * 16, 512)
        out_buf[FG + k] = blocks(dot(two_t[...], grad, 1, 0).astype(BF16))
        send(FG + k)

    @pl.loop(0, STEPS)
    def _(k):
        forward(MF + k + 1)
        arrived(MF + k)
        first = in_buf[MF + k].reshape(SEQ * 16, 512)
        out_buf[MX + k] = blocks(dot(two_v[...], first, 1, 0).astype(BF16))
        send(MX + k)
        part = dot(in_buf[MG + k].reshape(SEQ * 16, 512), first, 1, 1)
        grad_v[0, 0] += part[:, :256].reshape(ZH, PLANE, 16, 256)
        grad_v[0, 1] += part[:, 256:].reshape(ZH, PLANE, 16, 256)

    def pair_copy(m):
        return remote(grad_v.at[m, 1 - core], sib_v.at[m], sib_send.at[m], sib_recv.at[m], sibling)

    def plane_sends(m):
        pair_copy(m).wait_recv()
        sum_v[m] = grad_v[m, core] + sib_v[m]

        @pl.loop(1, PLANE)
        def _(d):
            to = plane_at(d)
            remote(
                sum_v.at[m, :, to], plane_v.at[m, at],
                pl_send.at[m], pl_recv.at[m], plane_dev(to),
            ).start()

        pltpu.make_async_copy(sum_v.at[m, :, at], plane_v.at[m, at], pl_recv.at[m]).start()

    def z_sends(m):
        drain(plane_v.at[m], pl_recv.at[m])
        zsend_v[m] = jnp.sum(plane_v[m], axis=0)

        @pl.loop(1, NZ)
        def _(d):
            to = (z + d) % NZ
            remote(
                zsend_v.at[m, to // ZL], zrecv_v.at[m, z],
                zz_send.at[m], zz_recv.at[m], z_dev(to),
            ).start()

        pltpu.make_async_copy(zsend_v.at[m, hi], zrecv_v.at[m, z], zz_recv.at[m]).start()

    def fin_copy(m):
        return remote(fin_v.at[m, core], fin_v.at[m, core], fin_send.at[m], fin_recv.at[m], sibling)

    def fin_other(m):
        return remote(
            fin_v.at[m, 1 - core], fin_v.at[m, 1 - core], fin_send.at[m], fin_recv.at[m], sibling
        )

    def finish(m):
        drain(zrecv_v.at[m], zz_recv.at[m])
        fin_v[m, core] = jnp.sum(zrecv_v[m], axis=0) * scales[m]
        fin_copy(m).start()

    pair_copy(0).start()
    plane_sends(0)

    def store(n, src, dst, k):
        return pltpu.make_async_copy(src.at[k], dst.at[:, k], store_sem.at[n, k])

    @pl.loop(0, STEPS)
    def _(k):
        forward(FG + k + 1)
        arrived(FG + k)
        fg = in_buf[FG + k].astype(F32)
        scaled = (fg * tw_v[...].astype(F32)[None]).astype(BF16)
        tw_add = jnp.sum(fg * pre_v[k], axis=0)
        tw_part[0] += tw_add[:, :256]
        tw_part[1] += tw_add[:, 256:]
        scaled = scaled.reshape(SEQ * 16, 512)
        vg_v[k] = blocks(dot(scaled, one_v[...], 1, 0).astype(BF16))
        store(0, vg_v, vg_hbm, k).start()
        part = dot(scaled, x_v[k].reshape(SEQ * 16, 512), 0, 0)
        grad_v[1, 0] += part[:, :256].reshape(ZH, PLANE, 16, 256)
        grad_v[1, 1] += part[:, 256:].reshape(ZH, PLANE, 16, 256)

    def tw_pair():
        return remote(tw_part.at[1 - core], tw_sib, tws_send, tws_recv, sibling)

    pair_copy(1).start()
    tw_pair().start()
    z_sends(0)
    plane_sends(1)
    tw_pair().wait_recv()
    tw_sum[...] = tw_part[core] + tw_sib[...]

    @pl.loop(1, ZL)
    def _(d):
        to = (lo + d) % ZL
        remote(
            tw_sum, tw_recv.at[lo], twz_send, twz_recv, (seq, to * NC + core)
        ).start()

    pltpu.make_async_copy(tw_sum, tw_recv.at[lo], twz_recv).start()
    z_sends(1)

    def gate(k):
        arrived(MX + k)
        gg_v[k] = (og_v[k].astype(F32) * in_buf[MX + k].astype(F32)).astype(BF16)
        store(1, gg_v, gg_hbm, k).start()

    @pl.loop(0, STEPS - 1)
    def _(k):
        forward(MX + k + 1)
        gate(k)

    finish(0)
    drain(tw_recv, twz_recv)
    fin_v[2, core] = jnp.sum(tw_recv[...], axis=0) * scales[2]
    fin_copy(2).start()
    finish(1)
    gate(STEPS - 1)

    for m, out in ((0, two_out), (2, tw_out), (1, one_out)):
        fin_other(m).wait_recv()
        out[:, :256] = fin_v[m, 0]
        out[:, 256:] = fin_v[m, 1]

    for k in range(STEPS):
        store(0, vg_v, vg_hbm, k).wait()
        store(1, gg_v, gg_hbm, k).wait()

    @pl.loop(0, 4 * STEPS)
    def _(i):
        across_copy(i).wait_send()
        drain(in_buf.at[i, pl.ds(0, PLANE - 1)], own_send.at[i])
        drain(in_buf.at[i, pl.ds(0, PLANE - 1)], fwd_send.at[i])

    for m in range(2):
        pair_copy(m).wait_send()
        drain(plane_v.at[m, pl.ds(0, PLANE - 1)], pl_send.at[m])
        drain(zrecv_v.at[m, pl.ds(0, NZ - 1)], zz_send.at[m])
    tw_pair().wait_send()
    drain(tw_recv.at[pl.ds(0, ZL - 1)], twz_send)
    for m in range(3):
        fin_copy(m).wait_send()


def body(seq_values, gate_values, out_grad, factor_one, factor_two, twiddle):
    width = seq_values.shape[0] * ZL * NC
    nblocks = factor_two.shape[0]
    block_len = factor_one.shape[0]
    scales = (
        1.0 / (width * block_len) ** 0.5,
        1.0 / (width * nblocks) ** 0.5,
        1.0 / width**0.5,
    )
    shape = (SEQ, STEPS, 16, 512)
    big = jax.ShapeDtypeStruct(shape, BF16)
    rows = jax.ShapeDtypeStruct((16, 512), F32)
    anywhere = pl.BlockSpec(memory_space=pl.ANY)
    vmem = pl.BlockSpec(memory_space=pltpu.VMEM)
    per_step = (STEPS, SEQ, 16, 512)
    dma = pltpu.SemaphoreType.DMA
    items = 4 * STEPS
    vg, gg, one, two, tw = pl.pallas_call(
        functools.partial(kernel, scales),
        out_shape=(big, big, rows, rows, rows),
        in_specs=[anywhere] * 6,
        out_specs=(anywhere, anywhere, vmem, vmem, vmem),
        scratch_shapes=[
            pltpu.VMEM(per_step, BF16),
            pltpu.VMEM(per_step, BF16),
            pltpu.VMEM(per_step, BF16),
            pltpu.VMEM((512, 512), BF16),
            pltpu.VMEM((512, 512), BF16),
            pltpu.VMEM((512, 512), BF16),
            pltpu.VMEM((16, 512), BF16),
            pltpu.VMEM(per_step, F32),
            pltpu.VMEM((items, SEQ, 16, 512), BF16),
            pltpu.VMEM((items, PLANE, 16, 512), BF16),
            pltpu.VMEM((items, SEQ, 16, 512), BF16),
            pltpu.VMEM(per_step, BF16),
            pltpu.VMEM(per_step, BF16),
            pltpu.VMEM((2, 2, ZH, PLANE, 16, 256), F32),
            pltpu.VMEM((2, ZH, PLANE, 16, 256), F32),
            pltpu.VMEM((2, ZH, PLANE, 16, 256), F32),
            pltpu.VMEM((2, PLANE, ZH, 16, 256), F32),
            pltpu.VMEM((2, ZH, 16, 256), F32),
            pltpu.VMEM((2, NZ, 16, 256), F32),
            pltpu.VMEM((2, 16, 256), F32),
            pltpu.VMEM((16, 256), F32),
            pltpu.VMEM((16, 256), F32),
            pltpu.VMEM((ZL, 16, 256), F32),
            pltpu.VMEM((3, 2, 16, 256), F32),
            dma((3, STEPS)), dma((3,)), dma((2, STEPS)),
            dma((items,)), dma((items,)), dma((items,)), dma((items,)), dma((items,)),
            dma((2,)), dma((2,)), dma((2,)), dma((2,)), dma((2,)), dma((2,)),
            dma(()), dma(()), dma(()), dma(()), dma((3,)), dma((3,)),
        ],
        compiler_params=pltpu.CompilerParams(
            collective_id=0, has_side_effects=True, vmem_limit_bytes=60 * 2**20
        ),
    )(
        seq_values.reshape(shape), gate_values.reshape(shape), out_grad.reshape(shape),
        factor_one, factor_two, twiddle,
    )
    whole = seq_values.shape
    return (vg.reshape(whole), gg.reshape(whole), one, two, tw)


def solution(mesh):
    return jax.shard_map(
        body,
        mesh=mesh,
        in_specs=(
            P("ch", "seq", None),
            P("ch", "seq", None),
            P("ch", "seq", None),
            P(),
            P(),
            P("seq", None),
        ),
        out_specs=(
            P("ch", "seq", None),
            P("ch", "seq", None),
            P("seq", None),
            P("seq", None),
            P("seq", None),
        ),
        check_vma=False,
    )
```

time: 729 us -> 213 us (0.29)
  waiting for transfers between devices: 554 us -> 0 us
  Pallas kernels: 0 us -> 206 us
  blocking collectives: 50.6 us -> 0 us
  local copies, waits for them, and re-layouts: 47.8 us -> 6.41 us
  matrix products: 29.3 us -> 0 us
  starting transfers between devices: 19.9 us -> 0 us
  between operations: 13.9 us -> 0.66 us
  other arithmetic: 11 us -> 0 us
    reduce_scatter x2 -> x0, waiting for transfers between devices: 440 us -> none  [the longest x1 228 us: body(): lax.psum_scatter(two_total, 'seq', scatter_dimension=0, tiled=True)]
    pallas_call x0 -> x1, Pallas kernels: none -> 206 us  [body(): pl.pallas_call(functools.partial(kernel, scales), out_shape=(big, big, ro...]
    psum x1 -> x0, waiting for transfers between devices: 79.8 us -> none  [body(): lax.psum((first_part, second_part, twiddle_part), 'ch')]
    all_to_all x1 -> x0, blocking collectives: 50.6 us -> none  [body(): lax.all_to_all(mixed_grad, 'seq', split_axis=2, concat_axis=1, tiled=True)]
    all_to_all x3 -> x0, waiting for transfers between devices: 34.5 us -> none  [the longest x1 20 us: body(): lax.all_to_all(block_grad, 'seq', split_axis=1, concat_axis=2, tiled=True)]
    dot_general x6 -> x0, matrix products: 29.3 us -> none  [the longest x1 7.51 us: body(): jnp.einsum('cbs,rs->cbr', seq_values, factor_one, preferred_element_type=...]
    convert_element_type x7 -> x0, local copies, waits for them, and re-layouts: 23.1 us -> none  [the longest x2 7.79 us: body(): first_grad_f = first_grad.astype(f32)]
    all_to_all x3 -> x0, starting transfers between devices: 19.6 us -> none  [the longest x1 9.04 us: body(): lax.all_to_all(mixed_across, 'seq', split_axis=1, concat_axis=2, tiled=True)]
  transfers between devices with their start and end apart: 6 -> 0, of which waited for: 5 -> 0; matrix products, arithmetic and copies ran while one was open for 5% -> 0% of each run, Pallas kernels for 0% -> 0%
where the time goes in v1:
time: 213 us
  Pallas kernels  206 us (97%)
  local copies, waits for them, and re-layouts  6.41 us (3%)
    pallas_call x1, Pallas kernels, body(): pl.pallas_call(functools.partial(kernel, scales), out_shape=(big, big, ro...  206 us
    unnamed x13, local copies, waits for them, and re-layouts  6.41 us

profile of v1, /device:TPU:1, one launch (start us, length us, event | category | flops | bytes accessed | tf_op | source)
XLA Modules:
  0.0 213.0 jit_solution(13896209131172640219)
XLA Ops:
  0.6 206.0 %shard_map.101 = (bf16[32,4,16,512]{3,2,1,0:T(8,128)(2,1)}, bf16[32,4,16,512]{3,2,1,0:T(8,128)(2,1)}, f32[16,512]{1,0:T(8,128)}, f32[16,512]{1,0:T(8,128)}, f32[16,512]{1,0:T(8,128)}) custom-call(bf16[32,4,16,512]{3,2,1,0:T(8,128)(2,1)} %bitcast.5, bf16[32,4,16,512]{3,2,1,0:T(8,128)(2,1)} %bitcast.6, bf16[32,4,16,512]{3,2,1,0:T(8,128)(2,1)} %bitcast.7, ...), custom_call_target="tpu_custom_call" | custom-call | tf_op jit(solution)/shard_map/pallas_call | solution.py:328
  206.6 0.0 copy-start
  206.6 3.2 %copy.16 = bf16[128,16,512]{2,1,0:T(8,128)(2,1)} copy(bf16[128,16,512]{2,1,0:T(8,128)(2,1)} %bitcast.9) | data formatting | bytes 4194304
  209.8 0.0 copy-done
  209.8 0.0 copy-start.3
  209.8 0.0 copy-start.2
  209.8 0.0 copy-start.1
  209.9 1.3 copy.17
  211.2 0.0 copy-done.3
  211.2 0.6 copy.18
  211.8 0.0 copy-done.2
  211.8 0.6 copy.19
  212.4 0.0 copy-done.1
  212.4 0.6 copy.20
Async XLA Ops:
  206.6 3.2 %copy-start = (bf16[32,4,16,512]{3,2,1,0:T(8,128)(2,1)S(1)}, bf16[32,4,16,512]{3,2,1,0:T(8,128)(2,1)}, u32[]{:S(2)}) copy-start(bf16[32,4,16,512]{3,2,1,0:T(8,128)(2,1)} %get-tuple-element.11) | copy-start | bytes 6291460
  209.8 1.3 copy-start.3
  209.8 1.9 copy-start.2
  209.8 2.6 %copy-start.1 = (f32[16,512]{1,0:T(8,128)S(1)}, f32[16,512]{1,0:T(8,128)}, u32[]{:S(2)}) copy-start(f32[16,512]{1,0:T(8,128)} %get-tuple-element.24) | copy-start | bytes 98308

commit v2 on v1

--- a/solution.py
+++ b/solution.py
@@ -25,13 +25,13 @@
 def kernel(
     scales,
     x_hbm, gate_hbm, og_hbm, one_hbm, two_hbm, tw_hbm,
-    vg_hbm, gg_hbm, one_out, two_out, tw_out,
+    vg_out, gg_out, fin_out,
     x_v, gate_v, og_v, one_v, two_v, two_t, tw_v, pre_v,
     out_buf, relay_buf, in_buf, vg_v, gg_v,
     grad_v, sib_v, sum_v, plane_v, zsend_v, zrecv_v,
     tw_part, tw_sib, tw_sum, tw_recv, fin_v,
-    load_sem, mat_sem, store_sem,
-    z_send, z_recv, own_send, fwd_send, in_recv,
+    load_sem, mat_sem, store_sem, keep_sem,
+    z_send, z_recv, own_send, fwd_send, in_recv, direct_send,
     sib_send, sib_recv, pl_send, pl_recv, zz_send, zz_recv,
     tws_send, tws_recv, twz_send, twz_recv, fin_send, fin_recv,
 ):
@@ -92,8 +92,12 @@
     def _(d):
         pl.semaphore_signal(barrier, inc=1, device_id=z_dev((z + d) % NZ), device_id_type=MESH)
 
+    @pl.loop(1, PLANE)
+    def _(d):
+        to = (other_hi * PLANE + plane_at(d), ch)
+        pl.semaphore_signal(barrier, inc=1, device_id=to, device_id_type=MESH)
+
     pl.semaphore_signal(barrier, inc=1, device_id=sibling, device_id_type=MESH)
-    pl.semaphore_wait(barrier, PLANE - 1 + NZ - 1 + 1)
 
     def across_copy(i):
         return remote(
@@ -101,9 +105,18 @@
             z_send.at[i], z_recv.at[i], across,
         )
 
-    def send(i):
+    def send_across(i):
         across_copy(i).start()
 
+    def send_direct(i):
+        @pl.loop(0, PLANE)
+        def _(d):
+            to = other_hi * PLANE + plane_at(d)
+            remote(
+                out_buf.at[i, to], in_buf.at[i, seq], direct_send, in_recv.at[i], (to, ch)
+            ).start()
+
+    def send_own(i):
         @pl.loop(1, PLANE)
         def _(d):
             to = plane_at(d)
@@ -142,7 +155,16 @@
         load(0, gate_hbm, gate_v, k).wait()
         load(1, og_hbm, og_v, k).wait()
         out_buf[MG + k] = (gate_v[k].astype(F32) * og_v[k].astype(F32)).astype(BF16)
-        send(MG + k)
+
+    pl.semaphore_wait(barrier, 2 * (PLANE - 1) + NZ - 1 + 1)
+
+    @pl.loop(MG, MG + STEPS)
+    def _(i):
+        send_across(i)
+
+    @pl.loop(MG, MG + STEPS)
+    def _(i):
+        send_own(i)
 
     mats[0].wait()
     mats[1].wait()
@@ -153,7 +175,8 @@
         pre = dot(x_v[k].reshape(SEQ * 16, 512), one_v[...], 1, 1)
         pre_v[k] = blocks(pre)
         out_buf[MF + k] = (blocks(pre) * tw_v[...].astype(F32)[None]).astype(BF16)
-        send(MF + k)
+        send_across(MF + k)
+        send_own(MF + k)
 
     mats[2].wait()
     two_t[...] = two_v[...].T
@@ -167,7 +190,8 @@
         arrived(MG + k)
         grad = in_buf[MG + k].reshape(SEQ * 16, 512)
         out_buf[FG + k] = blocks(dot(two_t[...], grad, 1, 0).astype(BF16))
-        send(FG + k)
+        send_across(FG + k)
+        send_own(FG + k)
 
     @pl.loop(0, STEPS)
     def _(k):
@@ -175,7 +199,12 @@
         arrived(MF + k)
         first = in_buf[MF + k].reshape(SEQ * 16, 512)
         out_buf[MX + k] = blocks(dot(two_v[...], first, 1, 0).astype(BF16))
-        send(MX + k)
+
+        @pl.when(k < STEPS - 1)
+        def _():
+            send_across(MX + k)
+
+        send_own(MX + k)
         part = dot(in_buf[MG + k].reshape(SEQ * 16, 512), first, 1, 1)
         grad_v[0, 0] += part[:, :256].reshape(ZH, PLANE, 16, 256)
         grad_v[0, 1] += part[:, 256:].reshape(ZH, PLANE, 16, 256)
@@ -199,7 +228,7 @@
 
     def z_sends(m):
         drain(plane_v.at[m], pl_recv.at[m])
-        zsend_v[m] = jnp.sum(plane_v[m], axis=0)
+        zsend_v[m] = jnp.sum(plane_v[m], axis=0).astype(BF16)
 
         @pl.loop(1, NZ)
         def _(d):
@@ -221,14 +250,14 @@
 
     def finish(m):
         drain(zrecv_v.at[m], zz_recv.at[m])
-        fin_v[m, core] = jnp.sum(zrecv_v[m], axis=0) * scales[m]
+        fin_v[m, core] = jnp.sum(zrecv_v[m].astype(F32), axis=0) * scales[m]
         fin_copy(m).start()
 
     pair_copy(0).start()
     plane_sends(0)
 
     def store(n, src, dst, k):
-        return pltpu.make_async_copy(src.at[k], dst.at[:, k], store_sem.at[n, k])
+        return pltpu.make_async_copy(src.at[k], dst.at[k], store_sem.at[n, k])
 
     @pl.loop(0, STEPS)
     def _(k):
@@ -241,7 +270,7 @@
         tw_part[1] += tw_add[:, 256:]
         scaled = scaled.reshape(SEQ * 16, 512)
         vg_v[k] = blocks(dot(scaled, one_v[...], 1, 0).astype(BF16))
-        store(0, vg_v, vg_hbm, k).start()
+        store(0, vg_v, vg_out, k).start()
         part = dot(scaled, x_v[k].reshape(SEQ * 16, 512), 0, 0)
         grad_v[1, 0] += part[:, :256].reshape(ZH, PLANE, 16, 256)
         grad_v[1, 1] += part[:, 256:].reshape(ZH, PLANE, 16, 256)
@@ -254,7 +283,7 @@
     z_sends(0)
     plane_sends(1)
     tw_pair().wait_recv()
-    tw_sum[...] = tw_part[core] + tw_sib[...]
+    tw_sum[...] = (tw_part[core] + tw_sib[...]).astype(BF16)
 
     @pl.loop(1, ZL)
     def _(d):
@@ -265,38 +294,46 @@
 
     pltpu.make_async_copy(tw_sum, tw_recv.at[lo], twz_recv).start()
     z_sends(1)
+    send_direct(MX + STEPS - 1)
 
     def gate(k):
         arrived(MX + k)
         gg_v[k] = (og_v[k].astype(F32) * in_buf[MX + k].astype(F32)).astype(BF16)
-        store(1, gg_v, gg_hbm, k).start()
-
-    @pl.loop(0, STEPS - 1)
+        store(1, gg_v, gg_out, k).start()
+
+    @pl.loop(0, STEPS - 2)
     def _(k):
         forward(MX + k + 1)
         gate(k)
 
+    gate(STEPS - 2)
+
     finish(0)
     drain(tw_recv, twz_recv)
-    fin_v[2, core] = jnp.sum(tw_recv[...], axis=0) * scales[2]
+    fin_v[2, core] = jnp.sum(tw_recv[...].astype(F32), axis=0) * scales[2]
     fin_copy(2).start()
     finish(1)
     gate(STEPS - 1)
 
-    for m, out in ((0, two_out), (2, tw_out), (1, one_out)):
+    for m in range(3):
         fin_other(m).wait_recv()
-        out[:, :256] = fin_v[m, 0]
-        out[:, 256:] = fin_v[m, 1]
+    keep = pltpu.make_async_copy(fin_v, fin_out, keep_sem)
+    keep.start()
+    keep.wait()
 
     for k in range(STEPS):
-        store(0, vg_v, vg_hbm, k).wait()
-        store(1, gg_v, gg_hbm, k).wait()
-
-    @pl.loop(0, 4 * STEPS)
+        store(0, vg_v, vg_out, k).wait()
+        store(1, gg_v, gg_out, k).wait()
+
+    @pl.loop(0, 4 * STEPS - 1)
     def _(i):
         across_copy(i).wait_send()
         drain(in_buf.at[i, pl.ds(0, PLANE - 1)], own_send.at[i])
         drain(in_buf.at[i, pl.ds(0, PLANE - 1)], fwd_send.at[i])
+
+    last = 4 * STEPS - 1
+    drain(in_buf.at[last, pl.ds(0, PLANE - 1)], own_send.at[last])
+    drain(in_buf.at[last, pl.ds(0, PLANE)], direct_send)
 
     for m in range(2):
         pair_copy(m).wait_send()
@@ -306,6 +343,25 @@
     drain(tw_recv.at[pl.ds(0, ZL - 1)], twz_send)
     for m in range(3):
         fin_copy(m).wait_send()
+
+
+def write_out(vg_in, gg_in, fin_in, vg, gg, two, one, tw, big_sem, fin_sem):
+    copies = [
+        pltpu.make_async_copy(src.at[k], dst.at[:, k], big_sem.at[n, k])
+        for k in range(STEPS)
+        for n, (src, dst) in enumerate(((vg_in, vg), (gg_in, gg)))
+    ]
+    copies += [
+        pltpu.make_async_copy(
+            fin_in.at[m, half], dst.at[:, pl.ds(half * 256, 256)], fin_sem.at[m, half]
+        )
+        for half in range(2)
+        for m, dst in enumerate((two, one, tw))
+    ]
+    for copy in copies:
+        copy.start()
+    for copy in copies:
+        copy.wait()
 
 
 def body(seq_values, gate_values, out_grad, factor_one, factor_two, twiddle):
@@ -321,15 +377,18 @@
     big = jax.ShapeDtypeStruct(shape, BF16)
     rows = jax.ShapeDtypeStruct((16, 512), F32)
     anywhere = pl.BlockSpec(memory_space=pl.ANY)
-    vmem = pl.BlockSpec(memory_space=pltpu.VMEM)
     per_step = (STEPS, SEQ, 16, 512)
     dma = pltpu.SemaphoreType.DMA
     items = 4 * STEPS
-    vg, gg, one, two, tw = pl.pallas_call(
+    kept = pl.pallas_call(
         functools.partial(kernel, scales),
-        out_shape=(big, big, rows, rows, rows),
+        out_shape=(
+            pltpu.VMEM(per_step, BF16),
+            pltpu.VMEM(per_step, BF16),
+            pltpu.VMEM((3, 2, 16, 256), F32),
+        ),
         in_specs=[anywhere] * 6,
-        out_specs=(anywhere, anywhere, vmem, vmem, vmem),
+        out_specs=(anywhere,) * 3,
         scratch_shapes=[
             pltpu.VMEM(per_step, BF16),
             pltpu.VMEM(per_step, BF16),
@@ -340,7 +399,7 @@
             pltpu.VMEM((16, 512), BF16),
             pltpu.VMEM(per_step, F32),
             pltpu.VMEM((items, SEQ, 16, 512), BF16),
-            pltpu.VMEM((items, PLANE, 16, 512), BF16),
+            pltpu.VMEM((items - 1, PLANE, 16, 512), BF16),
             pltpu.VMEM((items, SEQ, 16, 512), BF16),
             pltpu.VMEM(per_step, BF16),
             pltpu.VMEM(per_step, BF16),
@@ -348,25 +407,34 @@
             pltpu.VMEM((2, ZH, PLANE, 16, 256), F32),
             pltpu.VMEM((2, ZH, PLANE, 16, 256), F32),
             pltpu.VMEM((2, PLANE, ZH, 16, 256), F32),
-            pltpu.VMEM((2, ZH, 16, 256), F32),
-            pltpu.VMEM((2, NZ, 16, 256), F32),
+            pltpu.VMEM((2, ZH, 16, 256), BF16),
+            pltpu.VMEM((2, NZ, 16, 256), BF16),
             pltpu.VMEM((2, 16, 256), F32),
             pltpu.VMEM((16, 256), F32),
-            pltpu.VMEM((16, 256), F32),
-            pltpu.VMEM((ZL, 16, 256), F32),
+            pltpu.VMEM((16, 256), BF16),
+            pltpu.VMEM((ZL, 16, 256), BF16),
             pltpu.VMEM((3, 2, 16, 256), F32),
-            dma((3, STEPS)), dma((3,)), dma((2, STEPS)),
-            dma((items,)), dma((items,)), dma((items,)), dma((items,)), dma((items,)),
+            dma((3, STEPS)), dma((3,)), dma((2, STEPS)), dma(()),
+            dma((items - 1,)), dma((items - 1,)), dma((items,)), dma((items - 1,)), dma((items,)),
+            dma(()),
             dma((2,)), dma((2,)), dma((2,)), dma((2,)), dma((2,)), dma((2,)),
             dma(()), dma(()), dma(()), dma(()), dma((3,)), dma((3,)),
         ],
         compiler_params=pltpu.CompilerParams(
-            collective_id=0, has_side_effects=True, vmem_limit_bytes=60 * 2**20
+            collective_id=0, has_side_effects=True, vmem_limit_bytes=50 * 2**20
         ),
     )(
         seq_values.reshape(shape), gate_values.reshape(shape), out_grad.reshape(shape),
         factor_one, factor_two, twiddle,
     )
+    vg, gg, two, one, tw = pl.pallas_call(
+        write_out,
+        out_shape=(big, big, rows, rows, rows),
+        in_specs=[anywhere] * 3,
+        out_specs=(anywhere,) * 5,
+        scratch_shapes=[dma((2, STEPS)), dma((3, 2))],
+        compiler_params=pltpu.CompilerParams(vmem_limit_bytes=4 * 2**20),
+    )(*(pltpu.with_memory_space_constraint(part, pltpu.VMEM) for part in kept))
     whole = seq_values.shape
     return (vg.reshape(whole), gg.reshape(whole), one, two, tw)
 

time: 213 us -> 205 us (0.962)
  local copies, waits for them, and re-layouts: 6.41 us -> 0 us
    unnamed x13 -> x0, local copies, waits for them, and re-layouts: 6.41 us -> none
    pallas_call x1 -> x2, Pallas kernels: 206 us -> 204 us  [the longest x1 202 us: body(): pl.pallas_call(functools.partial(kernel, scales), out_shape=(pltpu.VMEM(p...]
where the time goes in v2:
time: 205 us
  Pallas kernels  204 us (100%)
    pallas_call x1, Pallas kernels, body(): pl.pallas_call(functools.partial(kernel, scales), out_shape=(pltpu.VMEM(p...  202 us

profile of v2, /device:TPU:1, one launch (start us, length us, event | category | flops | bytes accessed | tf_op | source)
XLA Modules:
  0.0 204.5 jit_solution(13146399362740171952)
XLA Ops:
  0.6 201.7 %shard_map.101 = (bf16[4,32,16,512]{3,2,1,0:T(8,128)(2,1)S(1)}, bf16[4,32,16,512]{3,2,1,0:T(8,128)(2,1)S(1)}, f32[3,2,16,256]{3,2,1,0:T(8,128)S(1)}) custom-call(bf16[32,4,16,512]{3,2,1,0:T(8,128)(2,1)} %bitcast.5, bf16[32,4,16,512]{3,2,1,0:T(8,128)(2,1)} %bitcast.6, bf16[32,4,16,512]{3,2,1,0:T(8,128)(2,1)} %bitcast.7, bf16[512,512]{1,0:T(8,128)(2,1)} %one_hbm.1, ...), custom_call_target="tpu_custom_call" | custom-call | tf_op jit(solution)/shard_map/pallas_call | solution.py:383
  202.4 2.2 %shard_map.102 = (bf16[32,4,16,512]{3,2,1,0:T(8,128)(2,1)}, bf16[32,4,16,512]{3,2,1,0:T(8,128)(2,1)}, f32[16,512]{1,0:T(8,128)}, f32[16,512]{1,0:T(8,128)}, f32[16,512]{1,0:T(8,128)}) custom-call(bf16[4,32,16,512]{3,2,1,0:T(8,128)(2,1)S(1)} %get-tuple-element.13.vg_in, bf16[4,32,16,512]{3,2,1,0:T(8,128)(2,1)S(1)} %get-tuple-element.14.gg_in, ...), custom_call_target="tpu_custom_call" | custom-call | tf_op jit(solution)/shard_map/pallas_call | solution.py:430

commit v3 on v2

--- a/solution.py
+++ b/solution.py
@@ -13,6 +13,7 @@
 NZ = ZH * ZL
 SEQ = ZH * PLANE
 STEPS = 4
+PARTS = 4
 MG, MF, FG, MX = 0, STEPS, 2 * STEPS, 3 * STEPS
 F32 = jnp.float32
 BF16 = jnp.bfloat16
@@ -27,10 +28,10 @@
     x_hbm, gate_hbm, og_hbm, one_hbm, two_hbm, tw_hbm,
     vg_out, gg_out, fin_out,
     x_v, gate_v, og_v, one_v, two_v, two_t, tw_v, pre_v,
-    out_buf, relay_buf, in_buf, vg_v, gg_v,
+    out_buf, relay_buf, in_buf,
     grad_v, sib_v, sum_v, plane_v, zsend_v, zrecv_v,
     tw_part, tw_sib, tw_sum, tw_recv, fin_v,
-    load_sem, mat_sem, store_sem, keep_sem,
+    load_sem, mat_sem, round_sem, go_sem,
     z_send, z_recv, own_send, fwd_send, in_recv, direct_send,
     sib_send, sib_recv, pl_send, pl_recv, zz_send, zz_recv,
     tws_send, tws_recv, twz_send, twz_recv, fin_send, fin_recv,
@@ -73,7 +74,73 @@
         pltpu.make_async_copy(two_hbm, two_v, mat_sem.at[2]),
     )
 
-    for k in range(STEPS):
+    load(0, gate_hbm, gate_v, 0).start()
+    load(1, og_hbm, og_v, 0).start()
+
+    is_hub = (px % 2 == lo // 2) & (py % 2 == lo % 2) & (core == 0)
+
+    def hub_at(h, bx, by, l):
+        return (h * PLANE + (2 * bx + l // 2) * NY + 2 * by + l % 2, l * NC)
+
+    bx, by = px // 2, py // 2
+    my_hub = hub_at(hi, bx, by, lo)
+    edges = (
+        hub_at(hi, 1 - bx, by, lo),
+        hub_at(hi, bx, 1 - by, lo),
+        hub_at(hi, bx, by, lo + 1 - 2 * (lo % 2)),
+        hub_at(hi, bx, by, (lo + 2) % ZL),
+        across,
+    )
+
+    def member(j):
+        mx = 2 * bx + (lo // 2 + j // 4) % 2
+        my = 2 * by + (lo + j // 2) % 2
+        return (hi * PLANE + mx * NY + my, lo * NC + j % 2)
+
+    def tell(sem, dev):
+        pl.semaphore_signal(sem, inc=1, device_id=dev, device_id_type=MESH)
+
+    barrier = pltpu.get_barrier_semaphore()
+    tell(barrier, across)
+
+    @pl.when(is_hub)
+    def _():
+        for dev in edges[:-1]:
+            tell(barrier, dev)
+
+        @pl.loop(1, 8)
+        def _(j):
+            tell(barrier, member(j))
+
+    @pl.when(jnp.logical_not(is_hub))
+    def _():
+        tell(barrier, my_hub)
+
+    def enter():
+        @pl.when(is_hub)
+        def _():
+            pl.semaphore_wait(barrier, 1 + len(edges) - 1 + 7)
+
+        @pl.when(jnp.logical_not(is_hub))
+        def _():
+            pl.semaphore_wait(barrier, 2)
+
+    def everyone_in():
+        @pl.when(is_hub)
+        def _():
+            for n, dev in enumerate(edges):
+                tell(round_sem.at[n], dev)
+                pl.semaphore_wait(round_sem.at[n], 1)
+
+            @pl.loop(1, 8)
+            def _(j):
+                tell(go_sem, member(j))
+
+        @pl.when(jnp.logical_not(is_hub))
+        def _():
+            pl.semaphore_wait(go_sem, 1)
+
+    for k in range(1, STEPS):
         load(0, gate_hbm, gate_v, k).start()
         load(1, og_hbm, og_v, k).start()
     mats[0].start()
@@ -82,22 +149,6 @@
         load(2, x_hbm, x_v, k).start()
     mats[2].start()
 
-    barrier = pltpu.get_barrier_semaphore()
-
-    @pl.loop(1, PLANE)
-    def _(d):
-        pl.semaphore_signal(barrier, inc=1, device_id=plane_dev(plane_at(d)), device_id_type=MESH)
-
-    @pl.loop(1, NZ)
-    def _(d):
-        pl.semaphore_signal(barrier, inc=1, device_id=z_dev((z + d) % NZ), device_id_type=MESH)
-
-    @pl.loop(1, PLANE)
-    def _(d):
-        to = (other_hi * PLANE + plane_at(d), ch)
-        pl.semaphore_signal(barrier, inc=1, device_id=to, device_id_type=MESH)
-
-    pl.semaphore_signal(barrier, inc=1, device_id=sibling, device_id_type=MESH)
 
     def across_copy(i):
         return remote(
@@ -150,21 +201,19 @@
     def blocks(value):
         return value.reshape(SEQ, 16, 512)
 
-    @pl.loop(0, STEPS)
-    def _(k):
+    def grad_at_home(k):
         load(0, gate_hbm, gate_v, k).wait()
         load(1, og_hbm, og_v, k).wait()
         out_buf[MG + k] = (gate_v[k].astype(F32) * og_v[k].astype(F32)).astype(BF16)
 
-    pl.semaphore_wait(barrier, 2 * (PLANE - 1) + NZ - 1 + 1)
-
-    @pl.loop(MG, MG + STEPS)
-    def _(i):
-        send_across(i)
-
-    @pl.loop(MG, MG + STEPS)
-    def _(i):
-        send_own(i)
+    grad_at_home(0)
+    enter()
+    send_across(MG)
+
+    @pl.loop(1, STEPS)
+    def _(k):
+        grad_at_home(k)
+        send_across(MG + k)
 
     mats[0].wait()
     mats[1].wait()
@@ -176,7 +225,12 @@
         pre_v[k] = blocks(pre)
         out_buf[MF + k] = (blocks(pre) * tw_v[...].astype(F32)[None]).astype(BF16)
         send_across(MF + k)
-        send_own(MF + k)
+
+    everyone_in()
+
+    @pl.loop(MG, MF + STEPS)
+    def _(i):
+        send_own(i)
 
     mats[2].wait()
     two_t[...] = two_v[...].T
@@ -256,12 +310,12 @@
     pair_copy(0).start()
     plane_sends(0)
 
-    def store(n, src, dst, k):
-        return pltpu.make_async_copy(src.at[k], dst.at[k], store_sem.at[n, k])
-
     @pl.loop(0, STEPS)
     def _(k):
-        forward(FG + k + 1)
+        @pl.when(k < STEPS - 1)
+        def _():
+            forward(FG + k + 1)
+
         arrived(FG + k)
         fg = in_buf[FG + k].astype(F32)
         scaled = (fg * tw_v[...].astype(F32)[None]).astype(BF16)
@@ -269,8 +323,7 @@
         tw_part[0] += tw_add[:, :256]
         tw_part[1] += tw_add[:, 256:]
         scaled = scaled.reshape(SEQ * 16, 512)
-        vg_v[k] = blocks(dot(scaled, one_v[...], 1, 0).astype(BF16))
-        store(0, vg_v, vg_out, k).start()
+        vg_out[:, k] = blocks(dot(scaled, one_v[...], 1, 0).astype(BF16))
         part = dot(scaled, x_v[k].reshape(SEQ * 16, 512), 0, 0)
         grad_v[1, 0] += part[:, :256].reshape(ZH, PLANE, 16, 256)
         grad_v[1, 1] += part[:, 256:].reshape(ZH, PLANE, 16, 256)
@@ -281,6 +334,7 @@
     pair_copy(1).start()
     tw_pair().start()
     z_sends(0)
+    send_direct(MX + STEPS - 1)
     plane_sends(1)
     tw_pair().wait_recv()
     tw_sum[...] = (tw_part[core] + tw_sib[...]).astype(BF16)
@@ -293,13 +347,12 @@
         ).start()
 
     pltpu.make_async_copy(tw_sum, tw_recv.at[lo], twz_recv).start()
+    forward(MX)
     z_sends(1)
-    send_direct(MX + STEPS - 1)
 
     def gate(k):
         arrived(MX + k)
-        gg_v[k] = (og_v[k].astype(F32) * in_buf[MX + k].astype(F32)).astype(BF16)
-        store(1, gg_v, gg_out, k).start()
+        gg_out[:, k] = (og_v[k].astype(F32) * in_buf[MX + k].astype(F32)).astype(BF16)
 
     @pl.loop(0, STEPS - 2)
     def _(k):
@@ -317,13 +370,7 @@
 
     for m in range(3):
         fin_other(m).wait_recv()
-    keep = pltpu.make_async_copy(fin_v, fin_out, keep_sem)
-    keep.start()
-    keep.wait()
-
-    for k in range(STEPS):
-        store(0, vg_v, vg_out, k).wait()
-        store(1, gg_v, gg_out, k).wait()
+    fin_out[...] = fin_v[...]
 
     @pl.loop(0, 4 * STEPS - 1)
     def _(i):
@@ -346,9 +393,12 @@
 
 
 def write_out(vg_in, gg_in, fin_in, vg, gg, two, one, tw, big_sem, fin_sem):
+    part = SEQ // PARTS
     copies = [
-        pltpu.make_async_copy(src.at[k], dst.at[:, k], big_sem.at[n, k])
-        for k in range(STEPS)
+        pltpu.make_async_copy(
+            src.at[pl.ds(k * part, part)], dst.at[pl.ds(k * part, part)], big_sem.at[n, k]
+        )
+        for k in range(PARTS)
         for n, (src, dst) in enumerate(((vg_in, vg), (gg_in, gg)))
     ]
     copies += [
@@ -383,12 +433,12 @@
     kept = pl.pallas_call(
         functools.partial(kernel, scales),
         out_shape=(
-            pltpu.VMEM(per_step, BF16),
-            pltpu.VMEM(per_step, BF16),
+            pltpu.VMEM(shape, BF16),
+            pltpu.VMEM(shape, BF16),
             pltpu.VMEM((3, 2, 16, 256), F32),
         ),
         in_specs=[anywhere] * 6,
-        out_specs=(anywhere,) * 3,
+        out_specs=(pl.BlockSpec(memory_space=pltpu.VMEM),) * 3,
         scratch_shapes=[
             pltpu.VMEM(per_step, BF16),
             pltpu.VMEM(per_step, BF16),
@@ -401,8 +451,6 @@
             pltpu.VMEM((items, SEQ, 16, 512), BF16),
             pltpu.VMEM((items - 1, PLANE, 16, 512), BF16),
             pltpu.VMEM((items, SEQ, 16, 512), BF16),
-            pltpu.VMEM(per_step, BF16),
-            pltpu.VMEM(per_step, BF16),
             pltpu.VMEM((2, 2, ZH, PLANE, 16, 256), F32),
             pltpu.VMEM((2, ZH, PLANE, 16, 256), F32),
             pltpu.VMEM((2, ZH, PLANE, 16, 256), F32),
@@ -414,7 +462,8 @@
             pltpu.VMEM((16, 256), BF16),
             pltpu.VMEM((ZL, 16, 256), BF16),
             pltpu.VMEM((3, 2, 16, 256), F32),
-            dma((3, STEPS)), dma((3,)), dma((2, STEPS)), dma(()),
+            dma((3, STEPS)), dma((3,)),
+            pltpu.SemaphoreType.REGULAR((5,)), pltpu.SemaphoreType.REGULAR,
             dma((items - 1,)), dma((items - 1,)), dma((items,)), dma((items - 1,)), dma((items,)),
             dma(()),
             dma((2,)), dma((2,)), dma((2,)), dma((2,)), dma((2,)), dma((2,)),
@@ -432,7 +481,7 @@
         out_shape=(big, big, rows, rows, rows),
         in_specs=[anywhere] * 3,
         out_specs=(anywhere,) * 5,
-        scratch_shapes=[dma((2, STEPS)), dma((3, 2))],
+        scratch_shapes=[dma((2, PARTS)), dma((3, 2))],
         compiler_params=pltpu.CompilerParams(vmem_limit_bytes=4 * 2**20),
     )(*(pltpu.with_memory_space_constraint(part, pltpu.VMEM) for part in kept))
     whole = seq_values.shape

time: 205 us -> 202 us (0.985)
  Pallas kernels: 204 us -> 201 us
    pallas_call x1, Pallas kernels: 202 us -> 199 us  [body(): pl.pallas_call(functools.partial(kernel, scales), out_shape=(pltpu.VMEM(s...]
where the time goes in v3:
time: 202 us
  Pallas kernels  201 us (100%)
    pallas_call x1, Pallas kernels, body(): pl.pallas_call(functools.partial(kernel, scales), out_shape=(pltpu.VMEM(s...  199 us

profile of v3, /device:TPU:1, one launch (start us, length us, event | category | flops | bytes accessed | tf_op | source)
XLA Modules:
  0.0 202.0 jit_solution(4915804914209261305)
XLA Ops:
  0.6 199.2 %shard_map.101 = (bf16[32,4,16,512]{3,2,1,0:T(8,128)(2,1)S(1)}, bf16[32,4,16,512]{3,2,1,0:T(8,128)(2,1)S(1)}, f32[3,2,16,256]{3,2,1,0:T(8,128)S(1)}) custom-call(bf16[32,4,16,512]{3,2,1,0:T(8,128)(2,1)} %bitcast.5, bf16[32,4,16,512]{3,2,1,0:T(8,128)(2,1)} %bitcast.6, bf16[32,4,16,512]{3,2,1,0:T(8,128)(2,1)} %bitcast.7, bf16[512,512]{1,0:T(8,128)(2,1)} %one_hbm.1, ...), custom_call_target="tpu_custom_call" | custom-call | tf_op jit(solution)/shard_map/pallas_call | solution.py:433
  199.8 2.2 %shard_map.102 = (bf16[32,4,16,512]{3,2,1,0:T(8,128)(2,1)}, bf16[32,4,16,512]{3,2,1,0:T(8,128)(2,1)}, f32[16,512]{1,0:T(8,128)}, f32[16,512]{1,0:T(8,128)}, f32[16,512]{1,0:T(8,128)}) custom-call(bf16[32,4,16,512]{3,2,1,0:T(8,128)(2,1)S(1)} %get-tuple-element.13.vg_in, bf16[32,4,16,512]{3,2,1,0:T(8,128)(2,1)S(1)} %get-tuple-element.14.gg_in, ...), custom_call_target="tpu_custom_call" | custom-call | tf_op jit(solution)/shard_map/pallas_call | solution.py:479

commit v4 on v3

--- a/solution.py
+++ b/solution.py
@@ -359,6 +359,21 @@
         forward(MX + k + 1)
         gate(k)
 
+    def sent(i):
+        across_copy(i).wait_send()
+        drain(in_buf.at[i, pl.ds(0, PLANE - 1)], own_send.at[i])
+        drain(in_buf.at[i, pl.ds(0, PLANE - 1)], fwd_send.at[i])
+
+    @pl.loop(0, MX + STEPS - 2)
+    def _(i):
+        sent(i)
+
+    for m in range(2):
+        pair_copy(m).wait_send()
+        drain(plane_v.at[m, pl.ds(0, PLANE - 1)], pl_send.at[m])
+    drain(zrecv_v.at[0, pl.ds(0, NZ - 1)], zz_send.at[0])
+    tw_pair().wait_send()
+
     gate(STEPS - 2)
 
     finish(0)
@@ -372,21 +387,12 @@
         fin_other(m).wait_recv()
     fin_out[...] = fin_v[...]
 
-    @pl.loop(0, 4 * STEPS - 1)
-    def _(i):
-        across_copy(i).wait_send()
-        drain(in_buf.at[i, pl.ds(0, PLANE - 1)], own_send.at[i])
-        drain(in_buf.at[i, pl.ds(0, PLANE - 1)], fwd_send.at[i])
-
+    sent(MX + STEPS - 2)
     last = 4 * STEPS - 1
     drain(in_buf.at[last, pl.ds(0, PLANE - 1)], own_send.at[last])
     drain(in_buf.at[last, pl.ds(0, PLANE)], direct_send)
 
-    for m in range(2):
-        pair_copy(m).wait_send()
-        drain(plane_v.at[m, pl.ds(0, PLANE - 1)], pl_send.at[m])
-        drain(zrecv_v.at[m, pl.ds(0, NZ - 1)], zz_send.at[m])
-    tw_pair().wait_send()
+    drain(zrecv_v.at[1, pl.ds(0, NZ - 1)], zz_send.at[1])
     drain(tw_recv.at[pl.ds(0, ZL - 1)], twz_send)
     for m in range(3):
         fin_copy(m).wait_send()

time: 202 us -> 202 us (level)
  no operation moved by 1% of the time
where the time goes in v4:
time: 202 us
  Pallas kernels  201 us (100%)
    pallas_call x1, Pallas kernels, body(): pl.pallas_call(functools.partial(kernel, scales), out_shape=(pltpu.VMEM(s...  199 us

profile of v4, /device:TPU:1, one launch (start us, length us, event | category | flops | bytes accessed | tf_op | source)
XLA Modules:
  0.0 201.9 jit_solution(10222771957691311957)
XLA Ops:
  0.6 199.1 %shard_map.101 = (bf16[32,4,16,512]{3,2,1,0:T(8,128)(2,1)S(1)}, bf16[32,4,16,512]{3,2,1,0:T(8,128)(2,1)S(1)}, f32[3,2,16,256]{3,2,1,0:T(8,128)S(1)}) custom-call(bf16[32,4,16,512]{3,2,1,0:T(8,128)(2,1)} %bitcast.5, bf16[32,4,16,512]{3,2,1,0:T(8,128)(2,1)} %bitcast.6, bf16[32,4,16,512]{3,2,1,0:T(8,128)(2,1)} %bitcast.7, bf16[512,512]{1,0:T(8,128)(2,1)} %one_hbm.1, ...), custom_call_target="tpu_custom_call" | custom-call | tf_op jit(solution)/shard_map/pallas_call | solution.py:439
  199.7 2.2 %shard_map.102 = (bf16[32,4,16,512]{3,2,1,0:T(8,128)(2,1)}, bf16[32,4,16,512]{3,2,1,0:T(8,128)(2,1)}, f32[16,512]{1,0:T(8,128)}, f32[16,512]{1,0:T(8,128)}, f32[16,512]{1,0:T(8,128)}) custom-call(bf16[32,4,16,512]{3,2,1,0:T(8,128)(2,1)S(1)} %get-tuple-element.13.vg_in, bf16[32,4,16,512]{3,2,1,0:T(8,128)(2,1)S(1)} %get-tuple-element.14.gg_in, ...), custom_call_target="tpu_custom_call" | custom-call | tf_op jit(solution)/shard_map/pallas_call | solution.py:485
